TPU v7x, 512 devices: a whole 4x4x16 slice. The times are simulated.
512 devices in a mesh: dp: 32 (over y_lo, z), tensor: 16 (over y_hi, x, core).
Axes of the slice: x: 4, y: 4 (y_hi: 2, y_lo: 2; y = y_hi * 2 + y_lo), z: 16, core: 2. Of those that a mesh axis runs over, the one named last changes fastest.
Arguments:
- tokens: bfloat16 [8192, 6144], P(('dp', 'tensor')), may hold values from -6 to 6
- layer_norm_gain: float32 [6144], replicated, may hold values from 0.5 to 1.5
- input_weight: bfloat16 [6144, 12288], P('dp', 'tensor'), may hold values from -0.078125 to 0.078125
- adapter_down_weight: bfloat16 [8, 6144], replicated, may hold values from -0.078125 to 0.078125
- adapter_up_weight: bfloat16 [8, 12288], P(None, 'tensor'), may hold values from -1 to 1
- output_gradient: bfloat16 [8192, 6144], P(('dp', 'tensor')), may hold values from -6 to 6
- attention_gradient: bfloat16 [8192, 4096], P('dp', 'tensor'), may hold values from -6 to 6
Outputs:
- token_gradient: bfloat16 [8192, 6144], P(('dp', 'tensor'))
- grad_a: float32 [8, 6144], replicated
- grad_b: float32 [8, 12288], P(None, 'tensor')
All inputs are finite; a program needn't handle non-finite values.
Results may differ from a plain program's by a relative error of at most 0.018.
Values may be sent and summed in bfloat16 or wider, within the bound.
A program may use at most 64 MiB of HBM per device.

v0:
```python
import jax
import jax.numpy as jnp
from jax import lax
from jax.sharding import PartitionSpec as P

HEAD = 128
HEADS_DEV = 2
SEQ = 256


EPSILON = 1e-06


def row_norm_value(values):
    row_mean = jnp.mean(values, axis=-1, keepdims=True)
    centred = values - row_mean
    inverse_norm = lax.rsqrt(jnp.mean(centred * centred, axis=-1, keepdims=True) + EPSILON)
    return (centred * inverse_norm, inverse_norm)


def layer_norm_backward(gradient, normal, inverse_norm):
    return (
        gradient
        - jnp.mean(gradient, axis=-1, keepdims=True)
        - normal * jnp.mean(gradient * normal, axis=-1, keepdims=True)
    ) * inverse_norm


def contract_trailing(first_op, second_op):
    return lax.dot_general(
        first_op, second_op, (((1,), (1,)), ((), ())), preferred_element_type=jnp.float32
    )


def contract_first(first_op, second_op):
    return lax.dot_general(
        first_op, second_op, (((0,), (0,)), ((), ())), preferred_element_type=jnp.float32
    )


def per_device(
    tokens,
    layer_norm_gain,
    input_weight,
    adapter_down_weight,
    adapter_up_weight,
    output_gradient,
    attention_gradient,
):
    local_rows = tokens.shape[0]
    head_span = HEADS_DEV * HEAD
    joined_cols = input_weight.shape[1]
    centred_normed_input, inverse_norm = row_norm_value(tokens.astype(jnp.float32))
    normed_input = (centred_normed_input * layer_norm_gain).astype(jnp.bfloat16)
    w_in_full = lax.all_gather(input_weight, "dp", axis=0, tiled=True)
    sharded_rows = lax.all_gather(normed_input, "tensor", axis=0, tiled=True)
    low_rank_slice = contract_trailing(sharded_rows, adapter_down_weight).astype(jnp.bfloat16)
    main_gradient = jnp.dot(sharded_rows, w_in_full, preferred_element_type=jnp.float32)
    main_gradient = main_gradient + jnp.dot(
        low_rank_slice, adapter_up_weight, preferred_element_type=jnp.float32
    )
    augmented = jnp.concatenate([main_gradient, low_rank_slice.astype(jnp.float32)], axis=1)
    joined_output = augmented[:, :joined_cols]
    low_rank_input = augmented[:, joined_cols:].astype(jnp.bfloat16)
    all_rows = joined_output.shape[0]
    images = all_rows // SEQ
    head_shape = (images, SEQ, HEADS_DEV, HEAD)
    query = joined_output[:, :head_span].reshape(head_shape)
    key_rows = joined_output[:, head_span : 2 * head_span].reshape(head_shape)
    value_round = joined_output[:, 2 * head_span :].reshape(head_shape).astype(jnp.bfloat16)
    query_norm, query_scale = row_norm_value(query)
    key_norm, key_scale = row_norm_value(key_rows)
    query_round = query_norm.astype(jnp.bfloat16)
    key_round = key_norm.astype(jnp.bfloat16)
    score_scale = HEAD ** (-0.5)
    scores = (
        jnp.einsum("bqhd,bkhd->bhqk", query_round, key_round, preferred_element_type=jnp.float32)
        * score_scale
    )
    weights = jnp.exp(scores)
    attn_probs = weights / jnp.sum(weights, axis=-1, keepdims=True)
    probs_round = attn_probs.astype(jnp.bfloat16)
    grad_att = attention_gradient.reshape(head_shape)
    grad_values = jnp.einsum(
        "bhqk,bqhd->bkhd", probs_round, grad_att, preferred_element_type=jnp.float32
    )
    grad_probs = jnp.einsum(
        "bqhd,bkhd->bhqk", grad_att, value_round, preferred_element_type=jnp.float32
    )
    grad_scores = attn_probs * (
        grad_probs - jnp.sum(attn_probs * grad_probs, axis=-1, keepdims=True)
    )
    scores_round = (grad_scores * score_scale).astype(jnp.bfloat16)
    grad_qn = jnp.einsum(
        "bhqk,bkhd->bqhd", scores_round, key_round, preferred_element_type=jnp.float32
    )
    grad_kn = jnp.einsum(
        "bhqk,bqhd->bkhd", scores_round, query_round, preferred_element_type=jnp.float32
    )
    grad_query = layer_norm_backward(grad_qn, query_norm, query_scale)
    grad_key = layer_norm_backward(grad_kn, key_norm, key_scale)
    part_shape = (all_rows, head_span)
    joined_gradient = jnp.concatenate(
        [
            grad_query.reshape(part_shape),
            grad_key.reshape(part_shape),
            grad_values.reshape(part_shape),
        ],
        axis=1,
    )
    joined_gradient = joined_gradient.astype(jnp.bfloat16)
    low_rank_gradient = lax.psum(
        contract_trailing(joined_gradient, adapter_up_weight), "tensor"
    ).astype(jnp.bfloat16)
    grad_b_part = contract_first(low_rank_input, joined_gradient)
    normed_gradient = lax.psum_scatter(
        contract_trailing(joined_gradient, w_in_full).astype(jnp.bfloat16),
        "tensor",
        scatter_dimension=0,
        tiled=True,
    ).astype(jnp.float32)
    own_start = lax.axis_index("tensor") * local_rows
    local_low_rank = lax.dynamic_slice_in_dim(low_rank_gradient, own_start, local_rows, 0)
    normed_gradient = normed_gradient + jnp.dot(
        local_low_rank, adapter_down_weight, preferred_element_type=jnp.float32
    )
    token_gradient = (
        output_gradient.astype(jnp.float32)
        + layer_norm_backward(normed_gradient * layer_norm_gain, centred_normed_input, inverse_norm)
    ).astype(jnp.bfloat16)
    grad_a_part = contract_first(local_low_rank, normed_input)
    factor = float(all_rows * lax.axis_size("dp")) ** (-0.5)
    grad_a = lax.psum(grad_a_part, ("dp", "tensor"))
    grad_b = lax.psum(grad_b_part, "dp")
    return (token_gradient, grad_a * factor, grad_b * factor)


def solution(mesh):
    placed = (
        P(("dp", "tensor"), None),
        P(),
        P("dp", "tensor"),
        P(),
        P(None, "tensor"),
        P(("dp", "tensor"), None),
        P("dp", "tensor"),
    )
    return jax.shard_map(
        per_device,
        mesh=mesh,
        in_specs=placed,
        out_specs=(P(("dp", "tensor"), None), P(), P(None, "tensor")),
        check_vma=False,
    )
```

profile of v0, /device:TPU:1, one launch (start us, length us, event | category | flops | bytes accessed | tf_op | source)
XLA Modules:
  0.0 834.6 jit_solution(12973953025344369059)
XLA Ops:
  7.2 1.1 convert_reduce_fusion
  8.3 1.2 fusion.22
  9.5 1.7 fusion.16
  11.3 0.7 all-gather.5.cloned.1.call-update
  12.1 1.0 copy.89
  13.1 72.3 %all-gather.3.cloned.1.call-done = bf16[256,6144]{1,0:T(8,128)(2,1)} async-done(((bf16[16,6144]{1,0:T(8,128)(2,1)}), bf16[256,6144]{1,0:T(8,128)(2,1)}) %all-gather.3.cloned.1.call-update) | async-done | bytes 3145744 | tf_op jit(solution)/shard_map/all_gather | solution.py:56
  85.4 2.9 convolution_convert_fusion.2
  88.3 130.8 %all-gather.5.cloned.1.call-done = bf16[6144,768]{1,0:T(8,128)(2,1)} async-done(((bf16[192,768]{1,0:T(8,128)(2,1)}), bf16[6144,768]{1,0:T(8,128)(2,1)}) %all-gather.5.cloned.1.call-update) | async-done | bytes 9437200 | tf_op jit(solution)/shard_map/all_gather | solution.py:55
  219.2 6.3 fusion.50
  225.5 0.3 convolution_add_fusion.1
  226.4 0.3 reduce_sum.128
  226.9 0.1 copy.67
  227.2 0.6 multiply_convert_fusion.3
  228.0 0.3 reduce_sum.130
  228.8 0.6 multiply_convert_fusion.2
  229.5 0.2 convolution_bitcast_fusion
  229.7 0.3 fusion.25
  230.1 0.3 fusion.43
  230.4 0.3 fusion.44
  230.7 0.3 fusion.2
  231.0 0.3 convolution_convert_fusion.1
  231.6 51.0 %psum.21 = bf16[256,8]{0,1:T(8,128)(2,1)S(1)} all-reduce(f32[256,8]{0,1:T(8,128)S(1)} %fusion.41), channel_id=1, replica_groups=mesh['dp'=32,'tensor'=16] {'tensor'}, use_global_device_ids=true, to_apply=%region_13.0 | all-reduce | flops 2048 | bytes 12288 | tf_op jit(solution)/shard_map/psum | solution.py:112
  282.6 0.9 fusion.31
  283.6 11.3 %convolution_convert_fusion = bf16[256,6144]{1,0:T(8,128)(2,1)} fusion(bf16[6144,768]{1,0:T(8,128)(2,1)} %all-gather.5.cloned.1.call-done, bf16[256,256]{0,1:T(8,128)(2,1)S(1)} %bitcast.64, bf16[256,256]{0,1:T(8,128)(2,1)S(1)} %bitcast.61, bf16[256,256]{0,1:T(8,128)(2,1)S(1)} %bitcast.58), kind=kOutput, calls=%fused_computation.1 | convolution fusion | flops 2418671616 | bytes 12976128 | tf_op jit(solution)/shard_map/dot_general | solution.py:30
  294.9 0.2 fusion.40
  295.1 93.0 %psum.23 = f32[8,768]{1,0:T(8,128)S(1)} all-reduce(f32[8,768]{1,0:T(8,128)S(1)} %fusion.40), channel_id=1, replica_groups=mesh['dp'=32,'tensor'=16] {'dp'}, use_global_device_ids=true, to_apply=%region_17.0 | all-reduce | flops 6144 | bytes 49152 | tf_op jit(solution)/shard_map/psum | solution.py:134
  388.1 0.6 broadcast_multiply_fusion.1
  388.8 340.0 %all-reduce.2.cloned.1.call-done = f32[8,6144]{1,0:T(8,128)} async-done(((f32[8,6144]{1,0:T(8,128)}), f32[8,6144]{1,0:T(8,128)}) %all-reduce.2.cloned.1.call-update) | async-done | bytes 196624 | tf_op jit(solution)/shard_map/psum | solution.py:133
  728.8 1.6 broadcast_multiply_fusion
  730.4 95.4 %reduce-scatter.2.cloned.1.call-done = bf16[16,6144]{1,0:T(8,128)(2,1)} async-done(((bf16[256,6144]{1,0:T(8,128)(2,1)}), bf16[16,6144]{1,0:T(8,128)(2,1)}) %reduce-scatter.2.cloned.1.call-update) | async-done | bytes 196624 | tf_op jit(solution)/shard_map/reduce_scatter | solution.py:116
  825.8 1.4 fusion.42
  827.2 0.9 fusion.21
  (48 shorter events, 2.1 us)
Async XLA Ops:
  7.2 78.2 %copy-start = (bf16[8,6144]{1,0:T(8,128)(2,1)S(1)}, bf16[8,6144]{1,0:T(8,128)(2,1)}, u32[]{:S(2)}) copy-start(bf16[8,6144]{1,0:T(8,128)(2,1)} %param.10) | copy-start | bytes 294916
  7.2 78.2 %all-gather.3.cloned.1.call-start = ((), (), s32[]{:S(2)}) async-start(), calls=%async_computation.1 | async-start | bytes 3342336 | tf_op jit(solution)/shard_map/all_gather | solution.py:56
  11.3 207.9 %all-gather.5.cloned.1.call-start = ((), (), s32[]{:S(2)}) async-start(), calls=%async_computation.2 | async-start | bytes 9732096 | tf_op jit(solution)/shard_map/all_gather | solution.py:55
  12.0 716.8 %all-reduce.2.cloned.1.call-start = ((), (), s32[]{:S(2)}) async-start(), calls=%async_computation.4 | async-start | bytes 393216 | tf_op jit(solution)/shard_map/psum | solution.py:133
  85.4 133.8 %copy-start.2 = (bf16[256,6144]{1,0:T(8,128)(2,1)S(1)}, bf16[256,6144]{1,0:T(8,128)(2,1)}, u32[]{:S(2)}) copy-start(bf16[256,6144]{1,0:T(8,128)(2,1)} %all-gather.3.cloned.1.call-done) | copy-start | bytes 9437188
  88.3 137.2 %copy-start.6 = (bf16[8,768]{1,0:T(8,128)(2,1)S(1)}, bf16[8,768]{1,0:T(8,128)(2,1)}, u32[]{:S(2)}) copy-start(bf16[8,768]{1,0:T(8,128)(2,1)} %param.11) | copy-start | bytes 36868
  230.4 52.2 %copy-start.3 = (bf16[16,6144]{1,0:T(8,128)(2,1)S(1)}, bf16[16,6144]{1,0:T(8,128)(2,1)}, u32[]{:S(2)}) copy-start(bf16[16,6144]{1,0:T(8,128)(2,1)} %fusion.16) | copy-start | bytes 589828
  283.5 542.3 %reduce-scatter.2.cloned.1.call-start = ((), (), s32[]{:S(2)}) async-start(), calls=%async_computation.3 | async-start | bytes 3342336 | tf_op jit(solution)/shard_map/reduce_scatter | solution.py:116
  294.9 530.9 %copy-start.1 = (bf16[16,6144]{1,0:T(8,128)(2,1)S(1)}, bf16[16,6144]{1,0:T(8,128)(2,1)}, u32[]{:S(2)}) copy-start(bf16[16,6144]{1,0:T(8,128)(2,1)} %param.7) | copy-start | bytes 589828
  294.9 530.9 %copy-start.5 = (f32[6144]{0:T(1024)S(1)}, f32[6144]{0:T(1024)}, u32[]{:S(2)}) copy-start(f32[6144]{0:T(1024)} %param.8) | copy-start | bytes 73732
  294.9 532.3 %copy-start.4 = (bf16[16,6144]{1,0:T(8,128)(2,1)S(1)}, bf16[16,6144]{1,0:T(8,128)(2,1)}, u32[]{:S(2)}) copy-start(bf16[16,6144]{1,0:T(8,128)(2,1)} %param.12) | copy-start | bytes 589828
Sparse Core Ops, SparseCore 0:
  11.9 73.4 all-gather.2
  87.4 131.6 all-gather.4
  283.6 445.0 all-reduce.1
  734.3 91.4 reduce-scatter.1
where the time goes:
time: 835 us
  waiting for transfers between devices  639 us (77%)
  blocking collectives  144 us (17%)
  matrix products  25.3 us (3%)
  between operations  14 us (2%)
  other arithmetic  9.3 us (1%)
    psum x1, waiting for transfers between devices, per_device(): grad_a = lax.psum(grad_a_part, ('dp', 'tensor'))  340 us
    all_gather x1, waiting for transfers between devices, per_device(): w_in_full = lax.all_gather(input_weight, 'dp', axis=0, tiled=True)  131 us
    reduce_scatter x1, waiting for transfers between devices, per_device(): lax.psum_scatter(contract_trailing(joined_gradient, w_in_full).astype(jnp...  95.4 us
    psum x1, blocking collectives, per_device(): grad_b = lax.psum(grad_b_part, 'dp')  93 us
    all_gather x1, waiting for transfers between devices, per_device(): sharded_rows = lax.all_gather(normed_input, 'tensor', axis=0, tiled=True)  72.3 us
    psum x1, blocking collectives, per_device(): lax.psum(contract_trailing(joined_gradient, adapter_up_weight), 'tensor')  51 us
  transfers between devices with their start and end apart: 4, of which 4 were waited for; matrix products, arithmetic and copies ran while one was open for 2% of the time, Pallas kernels for 0%

commit v1 on v0

v1 whole, which is shorter than its diff:
```python
import jax
import jax.numpy as jnp
from jax import lax
from jax.experimental import pallas as pl
from jax.experimental.pallas import tpu as pltpu
from jax.sharding import PartitionSpec as P

HEAD = 128
SEQ = 256
WIDTH = 6144
HALF = WIDTH // 2
RANK = 8
NZ = 16
ROWS = 192
COLS = 3 * HEAD
PARTS = 4
PART = HALF // PARTS
HP = PART // 2
PLANE = 512
EPSILON = 1e-06
F32 = jnp.float32
BF16 = jnp.bfloat16


def row_norm(values):
    mean = jnp.mean(values, axis=-1, keepdims=True)
    centred = values - mean
    inverse = lax.rsqrt(jnp.mean(centred * centred, axis=-1, keepdims=True) + EPSILON)
    return centred * inverse, inverse


def norm_backward(gradient, normal, inverse):
    return (
        gradient
        - jnp.mean(gradient, axis=-1, keepdims=True)
        - normal * jnp.mean(gradient * normal, axis=-1, keepdims=True)
    ) * inverse


def dot(a, b, ca=1, cb=0):
    return lax.dot_general(a, b, (((ca,), (cb,)), ((), ())), preferred_element_type=F32)


class Allocator:
    def __init__(self):
        self.size = 0

    def take(self, count):
        base = self.size
        self.size += count
        return base


def plan():
    al = Allocator()
    names = dict(
        wy=1, do=1, ring=32, t1=6, t2=6, t3=2,
        sib=2 * PARTS, r1=4 * PARTS, r2=4 * PARTS, r3=4 * PARTS, r4=4 * PARTS,
        g0=1, g1=3, g2=3, z1=3, z2=3, ax=3, ay=3, by=1,
    )
    bases = {name: al.take(count) for name, count in names.items()}
    return bases, al.size


SEM, N_SEM = plan()


def kernel(
    tok, gain, w, down, up, og, dout,
    o_tok, o_a, o_b,
    norm, wf, wst, acc, dall, xhat, inv, dpad, upad, lowr,
    gj, gl, sib_s, sib_r, own, part, r1, r2, tot, r3, r4, gn,
    gls, glx, gly, z1, z2, ga, gb,
    ssem, rsem,
):
    dp = lax.axis_index("dp")
    tt = lax.axis_index("tensor")
    yl, z = lax.div(dp, NZ), lax.rem(dp, NZ)
    yh = lax.div(tt, 8)
    x = lax.rem(lax.div(tt, 2), 4)
    c = lax.rem(tt, 2)
    y = 2 * yh + yl
    zh, zl = lax.div(z, 4), lax.rem(z, 4)
    other_c = 1 - c
    other_y = 1 - yl

    def at(y_, x_, z_, c_):
        return (
            lax.rem(y_, 2) * NZ + z_,
            lax.div(y_, 2) * 8 + x_ * 2 + c_,
        )

    xs = [at(y, lax.rem(x + d, 4), z, c) for d in (1, 2, 3)]
    ys = [at(lax.rem(y + d, 4), x, z, c) for d in (1, 2, 3)]
    zu = at(y, x, lax.rem(z + 1, NZ), c)
    zd = at(y, x, lax.rem(z + NZ - 1, NZ), c)
    zq = [at(y, x, zh * 4 + lax.rem(zl + d, 4), c) for d in (1, 2, 3)]
    zs = [at(y, x, lax.rem(zh + d, 4) * 4 + zl, c) for d in (1, 2, 3)]
    mate = at(y, x, z, other_c)
    pair = at(2 * yh + other_y, x, z, c)
    peers = [mate, *xs, *ys, zu, zd, *zq, *zs]

    def copy(src, dst, k, device):
        return pltpu.make_async_remote_copy(
            src_ref=src, dst_ref=dst, send_sem=ssem.at[k], recv_sem=rsem.at[k],
            device_id=device, device_id_type=pl.DeviceIdType.MESH,
        )

    pending = []

    def send(src, dst, k, device):
        one = copy(src, dst, k, device)
        one.start()
        pending.append(one)

    def arrived(ref, k):
        copy(ref, ref, k, mate).wait_recv()

    def flush(keep=0):
        while len(pending) > keep:
            pending.pop(0).wait_send()

    barrier = pltpu.get_barrier_semaphore()
    for device in peers:
        pl.semaphore_signal(barrier, inc=1, device_id=device, device_id_type=pl.DeviceIdType.MESH)

    for h in range(2):
        for j in range(3):
            wst[h, :, 128 * j : 128 * j + 128] = w[:, 256 * j + 128 * h : 256 * j + 128 * h + 128]
    wf[yl, z] = wst[yl]
    normal, inverse = row_norm(tok[...].astype(F32))
    xhat[...] = normal
    inv[...] = jnp.broadcast_to(inverse, inv.shape)
    norm[yl, yh, x, c] = (normal * gain[...]).astype(BF16)

    pl.semaphore_wait(barrier, len(peers))

    own_cols = pl.ds(pl.multiple_of(yl * HEAD, HEAD), HEAD)
    pair_cols = pl.ds(pl.multiple_of(other_y * HEAD, HEAD), HEAD)
    send(wst.at[other_y], wf.at[yl, z], SEM["wy"], pair)

    def ring_index(way, step, j):
        return SEM["ring"] + way * 16 + (step - 1) * 2 + j

    def ring_send(way, step, j):
        block = lax.rem(z + NZ - (step - 1), NZ) if way == 0 else lax.rem(z + step - 1, NZ)
        ref = wf.at[j, block]
        send(ref, ref, ring_index(way, step, j), zu if way == 0 else zd)

    def ring_wait(way, step, j):
        block = lax.rem(z + NZ - step, NZ) if way == 0 else lax.rem(z + step, NZ)
        arrived(wf.at[j, block], ring_index(way, step, j))

    for way in range(2):
        ring_send(way, 1, yl)
    a_cols, b_cols = pl.ds(0, HALF), pl.ds(HALF, HALF)
    a_ref = norm.at[yl, yh, x, c, :, a_cols]
    b_ref = norm.at[yl, yh, x, c, :, b_cols]
    for d in range(3):
        send(a_ref, a_ref, SEM["t1"] + d, xs[d])
        send(b_ref, b_ref, SEM["t1"] + 3 + d, ys[d])
    send(dout.at[:, pair_cols], dall.at[yl], SEM["do"], pair)
    dall[yl] = dout[:, own_cols]

    dpad[...] = jnp.concatenate([down[...].astype(F32), jnp.zeros((8, WIDTH), F32)], axis=0).astype(BF16)
    for j in range(3):
        cols = pl.ds(pl.multiple_of(256 * j + yl * HEAD, HEAD), HEAD)
        upad[:, 128 * j : 128 * j + 128] = jnp.concatenate(
            [up[:, cols].astype(F32), jnp.zeros((8, HEAD), F32)], axis=0
        ).astype(BF16)

    arrived(wf.at[other_y, z], SEM["wy"])
    for way in range(2):
        ring_send(way, 1, other_y)

    def forward(step):
        up_way = lax.rem(step + z, 2)
        base = lax.rem(up_way * (z + step - 1) + (1 - up_way) * (z - step + NZ), NZ)
        block = lax.div(base, 2)
        for j in range(2):
            lanes = pl.ds(pl.multiple_of(HALF * j + 2 * ROWS * block, 128), 2 * ROWS)
            left = norm[:, :, :, :, :, lanes].reshape(PLANE, 2 * ROWS)
            right = wf[j, pl.ds(2 * block, 2)].reshape(2 * ROWS, COLS)
            acc[...] += dot(left, right)

    def tokens_second():
        for d in range(3):
            xd, yd = lax.rem(x + 3 - d, 4), lax.rem(y + 3 - d, 4)
            arrived(norm.at[yl, yh, xd, c, :, a_cols], SEM["t1"] + d)
            arrived(norm.at[lax.rem(yd, 2), lax.div(yd, 2), x, c, :, b_cols], SEM["t1"] + 3 + d)
        ra = norm.at[yl, yh, :, c, :, a_cols]
        rb = norm.at[:, :, x, c, :, b_cols]
        for d in range(3):
            send(ra, ra, SEM["t2"] + d, ys[d])
            send(rb, rb, SEM["t2"] + 3 + d, xs[d])

    def tokens_mate():
        for d in range(3):
            yd = lax.rem(y + 3 - d, 4)
            arrived(norm.at[lax.rem(yd, 2), lax.div(yd, 2), :, c, :, a_cols], SEM["t2"] + d)
        ref = norm.at[:, :, :, c, :, a_cols]
        send(ref, ref, SEM["t3"], mate)
        for d in range(3):
            xd = lax.rem(x + 3 - d, 4)
            arrived(norm.at[:, :, xd, c, :, b_cols], SEM["t2"] + 3 + d)
        ref = norm.at[:, :, :, c, :, b_cols]
        send(ref, ref, SEM["t3"] + 1, mate)

    def tokens_done():
        arrived(norm.at[:, :, :, other_c, :, a_cols], SEM["t3"])
        arrived(norm.at[:, :, :, other_c, :, b_cols], SEM["t3"] + 1)

    for step in range(2, 9):
        if step < 8:
            for j in (yl, other_y):
                for way in range(2):
                    ring_wait(way, step - 1, j)
                    ring_send(way, step, j)
        else:
            ring_wait(0, 7, 0)
            ring_send(0, 8, 0)
            ring_wait(1, 7, 1)
            ring_send(1, 8, 1)
            ring_wait(0, 7, 1)
            ring_wait(1, 7, 0)
        if step == 2:
            tokens_second()
        if step == 5:
            tokens_mate()
        if step == 6:
            tokens_done()
            low = dot(norm[...].reshape(PLANE, WIDTH), dpad[...], 1, 1).astype(BF16)
            lowr[...] = low
            acc[...] = dot(low, upad[...])

            def several(s, carry):
                forward(s)
                return carry

            lax.fori_loop(1, 6, several, 0)
        if step == 7:
            forward(6)
        if step == 8:
            forward(7)
    arrived(dall.at[other_y], SEM["do"])
    flush(8)
    ring_wait(0, 8, 0)
    ring_wait(1, 8, 1)
    forward(8)

    scale = HEAD ** (-0.5)
    for i in range(2):
        rows = slice(SEQ * i, SEQ * i + SEQ)
        q_norm, q_inv = row_norm(acc[rows, 0:128])
        k_norm, k_inv = row_norm(acc[rows, 128:256])
        value = acc[rows, 256:384].astype(BF16)
        query, key = q_norm.astype(BF16), k_norm.astype(BF16)
        weights = jnp.exp(dot(query, key, 1, 1) * scale)
        probs = weights / jnp.sum(weights, axis=-1, keepdims=True)
        cot = dall[i]
        g_value = dot(probs.astype(BF16), cot, 0, 0)
        g_probs = dot(cot, value, 1, 1)
        g_scores = probs * (g_probs - jnp.sum(probs * g_probs, axis=-1, keepdims=True))
        g_scores = (g_scores * scale).astype(BF16)
        g_query = norm_backward(dot(g_scores, key), q_norm, q_inv)
        g_key = norm_backward(dot(g_scores, query, 0, 0), k_norm, k_inv)
        joined = jnp.concatenate([g_query, g_key, g_value], axis=1).astype(BF16)
        low = dot(joined, upad[...], 1, 1).astype(BF16)
        gls[c, :, SEQ * i : SEQ * i + SEQ] = dot(upad[...], joined, 1, 1)[0:RANK]
        if i == 0:
            b_part = dot(lowr[rows], joined, 0, 0)
        else:
            b_part = b_part + dot(lowr[rows], joined, 0, 0)
        for bh in range(2):
            for bx in range(4):
                for bc in range(2):
                    r = 16 * (8 * bh + 2 * bx + bc)
                    by = 2 * bh + i
                    rel = lax.rem(c + bc, 2)
                    gj[0, rel, bx, by] = joined[r : r + 16]
                    gj[1, rel, by, bx] = joined[r : r + 16]
                    gl[0, rel, bx, by] = low[r : r + 16]
                    gl[1, rel, by, bx] = low[r : r + 16]
    b_part = b_part[0:RANK]
    send(gls.at[c], gls.at[c], SEM["g0"], mate)

    place = [(x, y), (y, x)]
    near = [
        ((xs[0], xs[2]), (ys[0], ys[2])),
        ((ys[0], ys[2]), (xs[0], xs[2])),
    ]
    lo, hi = pl.ds(0, HP), pl.ds(HP, HP)

    def stage_product(i):
        for h in range(2):
            right = wf[h, 4 * i : 4 * i + 4].reshape(PART, COLS)
            low = dpad[:, HALF * h + PART * i : HALF * h + PART * i + PART]
            for rel in (1, 0):
                left = gj[h, rel].reshape(SEQ, COLS)
                out = dot(left, right, 1, 1) + dot(gl[h, rel].reshape(SEQ, 16), low)
                out = out.reshape(4, 4, 16, PART)
                if rel == 1:
                    sib_s[h, i] = out.astype(BF16)
                    send(sib_s.at[h, i], sib_r.at[h, i], SEM["sib"] + h * PARTS + i, mate)
                else:
                    own[h, i] = out

    def index(name, h, i, way):
        return SEM[name] + (h * PARTS + i) * 2 + way

    def stage_mate(i):
        for h in range(2):
            arrived(sib_r.at[h, i], SEM["sib"] + h * PARTS + i)
            part[h, i] = (own[h, i] + sib_r[h, i].astype(F32)).astype(BF16)
            far = lax.rem(place[h][0] + 2, 4)
            send(part.at[h, i, far, :, :, lo], r1.at[h, i, 0], index("r1", h, i, 0), near[h][0][0])
            send(part.at[h, i, far, :, :, hi], r1.at[h, i, 1], index("r1", h, i, 1), near[h][0][1])

    def stage_one(i):
        for h in range(2):
            me = place[h][0]
            nxt, prv = lax.rem(me + 1, 4), lax.rem(me + 3, 4)
            arrived(r1.at[h, i, 0], index("r1", h, i, 0))
            part[h, i, nxt, :, :, 0:HP] = (
                part[h, i, nxt, :, :, 0:HP].astype(F32) + r1[h, i, 0].astype(F32)
            ).astype(BF16)
            send(part.at[h, i, nxt], r2.at[h, i, 0], index("r2", h, i, 0), near[h][0][0])
            arrived(r1.at[h, i, 1], index("r1", h, i, 1))
            part[h, i, prv, :, :, HP:PART] = (
                part[h, i, prv, :, :, HP:PART].astype(F32) + r1[h, i, 1].astype(F32)
            ).astype(BF16)
            send(part.at[h, i, prv], r2.at[h, i, 1], index("r2", h, i, 1), near[h][0][1])

    def stage_two(i):
        for h in range(2):
            me, across = place[h]
            arrived(r2.at[h, i, 0], index("r2", h, i, 0))
            arrived(r2.at[h, i, 1], index("r2", h, i, 1))
            tot[h, i] = (
                part[h, i, me].astype(F32) + r2[h, i, 0].astype(F32) + r2[h, i, 1].astype(F32)
            ).astype(BF16)
            far = lax.rem(across + 2, 4)
            send(tot.at[h, i, far, :, lo], r3.at[h, i, 0], index("r3", h, i, 0), near[h][1][0])
            send(tot.at[h, i, far, :, hi], r3.at[h, i, 1], index("r3", h, i, 1), near[h][1][1])

    def stage_three(i):
        for h in range(2):
            me = place[h][1]
            nxt, prv = lax.rem(me + 1, 4), lax.rem(me + 3, 4)
            arrived(r3.at[h, i, 0], index("r3", h, i, 0))
            tot[h, i, nxt, :, 0:HP] = (
                tot[h, i, nxt, :, 0:HP].astype(F32) + r3[h, i, 0].astype(F32)
            ).astype(BF16)
            send(tot.at[h, i, nxt], r4.at[h, i, 0], index("r4", h, i, 0), near[h][1][0])
            arrived(r3.at[h, i, 1], index("r3", h, i, 1))
            tot[h, i, prv, :, HP:PART] = (
                tot[h, i, prv, :, HP:PART].astype(F32) + r3[h, i, 1].astype(F32)
            ).astype(BF16)
            send(tot.at[h, i, prv], r4.at[h, i, 1], index("r4", h, i, 1), near[h][1][1])

    def stage_four(i):
        for h in range(2):
            me = place[h][1]
            arrived(r4.at[h, i, 0], index("r4", h, i, 0))
            arrived(r4.at[h, i, 1], index("r4", h, i, 1))
            cols = slice(HALF * h + PART * i, HALF * h + PART * i + PART)
            gn[:, cols] = (
                tot[h, i, me].astype(F32) + r4[h, i, 0].astype(F32) + r4[h, i, 1].astype(F32)
            )

    factor = float(SEQ * 32) ** (-0.5)

    def spread(ref, slot, name, devices):
        for d in range(3):
            send(ref.at[slot], ref.at[slot], SEM[name] + d, devices[d])

    def gathered(ref, slot, name):
        for d in range(3):
            arrived(ref.at[lax.rem(slot + 3 - d, 4)], SEM[name] + d)

    def small(step):
        if step == 0:
            arrived(gls.at[other_c], SEM["g0"])
            glx[x] = gls[0] + gls[1]
            spread(glx, x, "g1", xs)
        if step == 1:
            gathered(glx, x, "g1")
            gly[y] = glx[0] + glx[1] + glx[2] + glx[3]
            spread(gly, y, "g2", ys)
        if step == 2:
            gathered(gly, y, "g2")
            low = gly[0] + gly[1] + gly[2] + gly[3]
            low = jnp.concatenate([low, jnp.zeros((8, PLANE), F32)], axis=0).astype(BF16)
            lanes = pl.ds(pl.multiple_of(384 * (4 * y + x), 128), 384)
            a_part = dot(low, norm[:, :, :, :, :, lanes].reshape(PLANE, 384))[0:RANK]
            z1[zl, 0:RANK] = a_part
            z1[zl, RANK : 2 * RANK] = b_part
            spread(z1, zl, "z1", zq)
        if step == 3:
            gathered(z1, zl, "z1")
            z2[zh] = z1[0] + z1[1] + z1[2] + z1[3]
            spread(z2, zh, "z2", zs)
        if step == 4:
            gathered(z2, zh, "z2")
            total = (z2[0] + z2[1] + z2[2] + z2[3]) * factor
            ga[y, x] = total[0:RANK]
            gb[yl] = total[RANK : 2 * RANK]
            send(gb.at[yl], gb.at[yl], SEM["by"], pair)
            for d in range(3):
                send(ga.at[y, x], ga.at[y, x], SEM["ax"] + d, xs[d])
        if step == 5:
            for d in range(3):
                arrived(ga.at[y, lax.rem(x + 3 - d, 4)], SEM["ax"] + d)
            spread(ga, y, "ay", ys)
        if step == 6:
            arrived(gb.at[other_y], SEM["by"])
            for h in range(2):
                for j in range(3):
                    o_b[:, 256 * j + 128 * h : 256 * j + 128 * h + 128] = gb[h, :, 128 * j : 128 * j + 128]
            gathered(ga, y, "ay")
            for a in range(4):
                for b in range(4):
                    k = 384 * (4 * a + b)
                    o_a[:, k : k + 384] = ga[a, b]

    stages = [stage_product, stage_mate, stage_one, stage_two, stage_three, stage_four]
    for t in range(PARTS + len(stages) - 1):
        for s in reversed(range(len(stages))):
            if 0 <= t - s < PARTS:
                stages[s](t - s)
        small(t)
        flush(24)

    gradient = gn[...] * gain[...]
    normal = xhat[...]
    out = norm_backward(gradient, normal, inv[:, 0:1])
    o_tok[...] = (og[...].astype(F32) + out).astype(BF16)
    flush()


def per_device(tokens, gain, weight, down, up, out_gradient, att_gradient):
    vmem = pl.BlockSpec(memory_space=pltpu.VMEM)
    shapes = [
        ((2, 2, 4, 2, 16, WIDTH), BF16),
        ((2, NZ, ROWS, COLS), BF16),
        ((2, ROWS, COLS), BF16),
        ((PLANE, COLS), F32),
        ((2, SEQ, HEAD), BF16),
        ((16, WIDTH), F32),
        ((16, HEAD), F32),
        ((16, WIDTH), BF16),
        ((16, COLS), BF16),
        ((PLANE, 16), BF16),
        ((2, 2, 4, 4, 16, COLS), BF16),
        ((2, 2, 4, 4, 16, 16), BF16),
        ((2, PARTS, 4, 4, 16, PART), BF16),
        ((2, PARTS, 4, 4, 16, PART), BF16),
        ((2, PARTS, 4, 4, 16, PART), F32),
        ((2, PARTS, 4, 4, 16, PART), BF16),
        ((2, PARTS, 2, 4, 16, HP), BF16),
        ((2, PARTS, 2, 4, 16, PART), BF16),
        ((2, PARTS, 4, 16, PART), BF16),
        ((2, PARTS, 2, 16, HP), BF16),
        ((2, PARTS, 2, 16, PART), BF16),
        ((16, WIDTH), F32),
        ((2, RANK, PLANE), F32),
        ((4, RANK, PLANE), F32),
        ((4, RANK, PLANE), F32),
        ((4, 2 * RANK, COLS), F32),
        ((4, 2 * RANK, COLS), F32),
        ((4, 4, RANK, 384), F32),
        ((2, RANK, COLS), F32),
    ]
    scratch = [pltpu.VMEM(shape, kind) for shape, kind in shapes]
    scratch += [pltpu.SemaphoreType.DMA((N_SEM,)), pltpu.SemaphoreType.DMA((N_SEM,))]
    return pl.pallas_call(
        kernel,
        out_shape=(
            jax.ShapeDtypeStruct((16, WIDTH), BF16),
            jax.ShapeDtypeStruct((RANK, WIDTH), F32),
            jax.ShapeDtypeStruct((RANK, 2 * COLS), F32),
        ),
        in_specs=[vmem] * 7,
        out_specs=(vmem, vmem, vmem),
        scratch_shapes=scratch,
        compiler_params=pltpu.CompilerParams(
            collective_id=0, has_side_effects=True, vmem_limit_bytes=52 * 1024 * 1024
        ),
    )(tokens, gain.reshape(1, WIDTH), weight, down, up, out_gradient, att_gradient)


def solution(mesh):
    placed = (
        P(("dp", "tensor"), None),
        P(),
        P("dp", "tensor"),
        P(),
        P(None, "tensor"),
        P(("dp", "tensor"), None),
        P("dp", "tensor"),
    )
    return jax.shard_map(
        per_device,
        mesh=mesh,
        in_specs=placed,
        out_specs=(P(("dp", "tensor"), None), P(), P(None, "tensor")),
        check_vma=False,
    )
```

time: 835 us -> 121 us (0.14)
  the two profiles are of different devices: /device:TPU:1 before, /device:TPU:32 now
where the time goes in v1:
time: 121 us; the launch traced here: 120 us
  Pallas kernels  112 us (93%)
  local copies, waits for them, and re-layouts  8.01 us (7%)
    pallas_call x1, Pallas kernels, per_device(): pl.pallas_call(kernel, out_shape=(jax.ShapeDtypeStruct((16, WIDTH), BF16)...  112 us
    unnamed x17, local copies, waits for them, and re-layouts  8.01 us

profile of v1, /device:TPU:32, one launch (start us, length us, event | category | flops | bytes accessed | tf_op | source)
XLA Modules:
  0.0 120.2 jit_solution(13804092136800141149)
XLA Ops:
  0.6 0.0 copy-start
  0.6 1.0 copy-done
  1.6 0.0 copy-start.1
  1.6 0.9 copy-done.1
  2.5 0.0 copy-start.2
  2.5 0.9 copy-done.2
  3.5 0.0 copy-start.3
  3.5 0.9 copy-done.3
  4.4 0.0 copy-start.4
  4.4 0.9 copy-done.4
  5.2 0.0 copy-start.5
  5.2 0.7 copy-done.5
  6.0 0.0 copy-start.6
  6.0 0.7 copy-done.6
  6.7 111.5 %shard_map.94 = (bf16[16,6144]{1,0:T(8,128)(2,1)S(1)}, f32[8,6144]{1,0:T(8,128)S(1)}, f32[8,768]{1,0:T(8,128)S(1)}) custom-call(bf16[16,6144]{1,0:T(8,128)(2,1)S(1)} %copy-done.1, f32[1,6144]{1,0:T(1,128)S(1)} %bitcast.1, bf16[192,768]{1,0:T(8,128)(2,1)S(1)} %copy-done, bf16[8,6144]{1,0:T(8,128)(2,1)S(1)} %copy-done.4, bf16[8,768]{1,0:T(8,128)(2,1)S(1)} %copy-done.6, ...), custom_call_target="tpu_custom_call" | custom-call | tf_op jit(solution)/shard_map/pallas_call | solution.py:476
  118.2 0.7 copy.13
  118.9 0.7 copy.14
  119.6 0.6 copy.15
Async XLA Ops:
  0.6 1.0 copy-start
  1.6 0.9 copy-start.1
  2.5 0.9 copy-start.2
  3.5 0.9 copy-start.3
  4.4 0.9 copy-start.4
  5.2 0.7 copy-start.5
  6.0 0.7 copy-start.6

commit v2 on v1

v2 whole, which is shorter than its diff:
```python
import jax
import jax.numpy as jnp
from jax import lax
from jax.experimental import pallas as pl
from jax.experimental.pallas import tpu as pltpu
from jax.sharding import PartitionSpec as P

HEAD = 128
SEQ = 256
WIDTH = 6144
HALF = WIDTH // 2
RANK = 8
NZ = 16
ROWS = 192
COLS = 3 * HEAD
PARTS = 4
PART = HALF // PARTS
HP = PART // 2
PLANE = 512
EPSILON = 1e-06
F32 = jnp.float32
BF16 = jnp.bfloat16


def row_norm(values):
    mean = jnp.mean(values, axis=-1, keepdims=True)
    centred = values - mean
    inverse = lax.rsqrt(jnp.mean(centred * centred, axis=-1, keepdims=True) + EPSILON)
    return centred * inverse, inverse


def norm_backward(gradient, normal, inverse):
    return (
        gradient
        - jnp.mean(gradient, axis=-1, keepdims=True)
        - normal * jnp.mean(gradient * normal, axis=-1, keepdims=True)
    ) * inverse


def dot(a, b, ca=1, cb=0):
    return lax.dot_general(a, b, (((ca,), (cb,)), ((), ())), preferred_element_type=F32)


class Allocator:
    def __init__(self):
        self.size = 0

    def take(self, count):
        base = self.size
        self.size += count
        return base


def plan():
    al = Allocator()
    names = dict(
        wy=3, do=1, ring=32, t1=6, t2=6, t3=2,
        sib=6 * PARTS, r1=4 * PARTS, r2=4 * PARTS, r3=6 * PARTS,
        g0=1, g1=3, g2=3, z1=3, z2=3, ax=15, by=1,
    )
    bases = {name: al.take(count) for name, count in names.items()}
    return bases, al.size


SEM, N_SEM = plan()


def kernel(
    tok_in, gain_in, w_in, down_in, up_in, og_in, dout_in,
    o_tok, o_a, o_b,
    tok, gain, down, up, og,
    norm, wf, acc, dall, xhat, inv, dpad, upad, lowr,
    gj, sib_s, sib_r, own, far, r1, beside, r2, tot, r3, gn,
    gls, glx, gly, z1, z2, ga, gb,
    ssem, rsem, lsem,
):
    dp = lax.axis_index("dp")
    tt = lax.axis_index("tensor")
    yl, z = lax.div(dp, NZ), lax.rem(dp, NZ)
    yh = lax.div(tt, 8)
    x = lax.rem(lax.div(tt, 2), 4)
    c = lax.rem(tt, 2)
    y = 2 * yh + yl
    zh, zl = lax.div(z, 4), lax.rem(z, 4)
    other_c = 1 - c
    other_y = 1 - yl

    def at(y_, x_, z_, c_):
        return (
            lax.rem(y_, 2) * NZ + z_,
            lax.div(y_, 2) * 8 + x_ * 2 + c_,
        )

    xs = [at(y, lax.rem(x + d, 4), z, c) for d in (1, 2, 3)]
    ys = [at(lax.rem(y + d, 4), x, z, c) for d in (1, 2, 3)]
    zu = at(y, x, lax.rem(z + 1, NZ), c)
    zd = at(y, x, lax.rem(z + NZ - 1, NZ), c)
    zq = [at(y, x, zh * 4 + lax.rem(zl + d, 4), c) for d in (1, 2, 3)]
    zs = [at(y, x, lax.rem(zh + d, 4) * 4 + zl, c) for d in (1, 2, 3)]
    mate = at(y, x, z, other_c)
    pair = at(2 * yh + other_y, x, z, c)
    plane = [(a, b) for a in range(4) for b in range(4) if a + b > 0]
    across = [at(lax.rem(y + a, 4), lax.rem(x + b, 4), z, c) for a, b in plane]
    peers = [mate, *across, zu, zd, *zq, *zs]

    def copy(src, dst, k, device):
        return pltpu.make_async_remote_copy(
            src_ref=src, dst_ref=dst, send_sem=ssem.at[k], recv_sem=rsem.at[k],
            device_id=device, device_id_type=pl.DeviceIdType.MESH,
        )

    pending = []

    def send(src, dst, k, device):
        one = copy(src, dst, k, device)
        one.start()
        pending.append(one)

    def arrived(ref, k):
        copy(ref, ref, k, mate).wait_recv()

    def flush(keep=0):
        while len(pending) > keep:
            pending.pop(0).wait_send()

    barrier = pltpu.get_barrier_semaphore()
    for device in peers:
        pl.semaphore_signal(barrier, inc=1, device_id=device, device_id_type=pl.DeviceIdType.MESH)

    own_cols = pl.ds(pl.multiple_of(yl * HEAD, HEAD), HEAD)
    pair_cols = pl.ds(pl.multiple_of(other_y * HEAD, HEAD), HEAD)
    locals_ = []

    def fetch(src, dst):
        one = pltpu.make_async_copy(src, dst, lsem.at[len(locals_)])
        one.start()
        locals_.append(one)
        return one

    get_w = []
    for j in range(3):
        cols = pl.ds(pl.multiple_of(256 * j + yl * HEAD, HEAD), HEAD)
        get_w.append(fetch(w_in.at[:, cols], wf.at[yl, z, :, pl.ds(128 * j, 128)]))
    get_tok = [fetch(tok_in, tok), fetch(gain_in, gain)]
    get_small = [fetch(down_in, down), fetch(up_in, up), fetch(dout_in.at[:, own_cols], dall.at[yl])]
    get_og = fetch(og_in, og)

    pl.semaphore_wait(barrier, len(peers))

    for j in range(3):
        cols = pl.ds(pl.multiple_of(256 * j + other_y * HEAD, HEAD), HEAD)
        send(w_in.at[:, cols], wf.at[yl, z, :, pl.ds(128 * j, 128)], SEM["wy"] + j, pair)
    for one in get_w:
        one.wait()

    def ring_index(way, step, j):
        return SEM["ring"] + way * 16 + (step - 1) * 2 + j

    def ring_send(way, step, j):
        block = lax.rem(z + NZ - (step - 1), NZ) if way == 0 else lax.rem(z + step - 1, NZ)
        ref = wf.at[j, block]
        send(ref, ref, ring_index(way, step, j), zu if way == 0 else zd)

    def ring_wait(way, step, j):
        block = lax.rem(z + NZ - step, NZ) if way == 0 else lax.rem(z + step, NZ)
        arrived(wf.at[j, block], ring_index(way, step, j))

    for way in range(2):
        ring_send(way, 1, yl)
    for one in get_tok:
        one.wait()
    normal, inverse = row_norm(tok[...].astype(F32))
    xhat[...] = normal
    inv[...] = jnp.broadcast_to(inverse, inv.shape)
    norm[yl, yh, x, c] = (normal * gain[...]).astype(BF16)

    a_cols, b_cols = pl.ds(0, HALF), pl.ds(HALF, HALF)
    a_ref = norm.at[yl, yh, x, c, :, a_cols]
    b_ref = norm.at[yl, yh, x, c, :, b_cols]
    for d in range(3):
        send(a_ref, a_ref, SEM["t1"] + d, xs[d])
        send(b_ref, b_ref, SEM["t1"] + 3 + d, ys[d])
    send(dout_in.at[:, pair_cols], dall.at[yl], SEM["do"], pair)
    for one in get_small:
        one.wait()

    dpad[...] = jnp.concatenate([down[...].astype(F32), jnp.zeros((8, WIDTH), F32)], axis=0).astype(BF16)
    for j in range(3):
        cols = pl.ds(pl.multiple_of(256 * j + yl * HEAD, HEAD), HEAD)
        upad[:, 128 * j : 128 * j + 128] = jnp.concatenate(
            [up[:, cols].astype(F32), jnp.zeros((8, HEAD), F32)], axis=0
        ).astype(BF16)

    for j in range(3):
        arrived(wf.at[other_y, z, :, pl.ds(128 * j, 128)], SEM["wy"] + j)
    for way in range(2):
        ring_send(way, 1, other_y)

    def forward(step):
        up_way = lax.rem(step + z, 2)
        base = lax.rem(up_way * (z + step - 1) + (1 - up_way) * (z - step + NZ), NZ)
        block = lax.div(base, 2)
        for j in range(2):
            lanes = pl.ds(pl.multiple_of(HALF * j + 2 * ROWS * block, 128), 2 * ROWS)
            left = norm[:, :, :, :, :, lanes].reshape(PLANE, 2 * ROWS)
            right = wf[j, pl.ds(2 * block, 2)].reshape(2 * ROWS, COLS)
            acc[...] += dot(left, right)

    def tokens_second():
        for d in range(3):
            xd, yd = lax.rem(x + 3 - d, 4), lax.rem(y + 3 - d, 4)
            arrived(norm.at[yl, yh, xd, c, :, a_cols], SEM["t1"] + d)
            arrived(norm.at[lax.rem(yd, 2), lax.div(yd, 2), x, c, :, b_cols], SEM["t1"] + 3 + d)
        ra = norm.at[yl, yh, :, c, :, a_cols]
        rb = norm.at[:, :, x, c, :, b_cols]
        for d in range(3):
            send(ra, ra, SEM["t2"] + d, ys[d])
            send(rb, rb, SEM["t2"] + 3 + d, xs[d])

    def tokens_mate():
        for d in range(3):
            yd = lax.rem(y + 3 - d, 4)
            arrived(norm.at[lax.rem(yd, 2), lax.div(yd, 2), :, c, :, a_cols], SEM["t2"] + d)
        ref = norm.at[:, :, :, c, :, a_cols]
        send(ref, ref, SEM["t3"], mate)
        for d in range(3):
            xd = lax.rem(x + 3 - d, 4)
            arrived(norm.at[:, :, xd, c, :, b_cols], SEM["t2"] + 3 + d)
        ref = norm.at[:, :, :, c, :, b_cols]
        send(ref, ref, SEM["t3"] + 1, mate)

    def tokens_done():
        arrived(norm.at[:, :, :, other_c, :, a_cols], SEM["t3"])
        arrived(norm.at[:, :, :, other_c, :, b_cols], SEM["t3"] + 1)

    def forward_first():
        low = dot(norm[...].reshape(PLANE, WIDTH), dpad[...], 1, 1).astype(BF16)
        lowr[...] = low
        acc[...] = dot(low, upad[...])

        def several(s, carry):
            forward(s)
            return carry

        lax.fori_loop(1, 6, several, 0)

    def ring_step(step):
        if step < 8:
            for j in (yl, other_y):
                for way in range(2):
                    ring_wait(way, step - 1, j)
                    ring_send(way, step, j)
        elif step == 8:
            ring_wait(0, 7, 0)
            ring_send(0, 8, 0)
            ring_wait(1, 7, 1)
            ring_send(1, 8, 1)
            ring_wait(0, 7, 1)
            ring_wait(1, 7, 0)
        else:
            ring_wait(0, 8, 0)
            ring_wait(1, 8, 1)

    def dout_done():
        arrived(dall.at[other_y], SEM["do"])
        flush(8)

    for step in range(2, 10):
        ring_step(step)
        if step == 2:
            tokens_second()
        if step == 5:
            tokens_mate()
        if step == 6:
            tokens_done()
            forward_first()
        if step == 7:
            forward(6)
        if step == 8:
            forward(7)
            dout_done()
        if step == 9:
            forward(8)

    def order(to, me):
        d = lax.rem(to - me + 6, 4)
        return lax.rem(2 * d, 5) - lax.div(d, 2) * (1 - lax.div(d, 3))

    scale = HEAD ** (-0.5)
    def attention():
        for i in range(2):
            rows = slice(SEQ * i, SEQ * i + SEQ)
            q_norm, q_inv = row_norm(acc[rows, 0:128])
            k_norm, k_inv = row_norm(acc[rows, 128:256])
            value = acc[rows, 256:384].astype(BF16)
            query, key = q_norm.astype(BF16), k_norm.astype(BF16)
            weights = jnp.exp(dot(query, key, 1, 1) * scale)
            probs = weights / jnp.sum(weights, axis=-1, keepdims=True)
            cot = dall[i]
            g_value = dot(probs.astype(BF16), cot, 0, 0)
            g_probs = dot(cot, value, 1, 1)
            g_scores = probs * (g_probs - jnp.sum(probs * g_probs, axis=-1, keepdims=True))
            g_scores = (g_scores * scale).astype(BF16)
            g_query = norm_backward(dot(g_scores, key), q_norm, q_inv)
            g_key = norm_backward(dot(g_scores, query, 0, 0), k_norm, k_inv)
            joined = jnp.concatenate([g_query, g_key, g_value], axis=1).astype(BF16)
            gls[c, :, SEQ * i : SEQ * i + SEQ] = dot(upad[...], joined, 1, 1)[0:RANK]
            if i == 0:
                b_part = dot(lowr[rows], joined, 0, 0)
            else:
                b_part = b_part + dot(lowr[rows], joined, 0, 0)
            for bh in range(2):
                for bx in range(4):
                    for bc in range(2):
                        r = 16 * (8 * bh + 2 * bx + bc)
                        by = 2 * bh + i
                        rel = lax.rem(c + bc, 2)
                        kx, ky = order(bx, x), order(by, y)
                        gj[0, rel, kx, ky] = joined[r : r + 16]
                        gj[1, rel, ky, kx] = joined[r : r + 16]
        return b_part[0:RANK]

    b_part = attention()
    send(gls.at[c], gls.at[c], SEM["g0"], mate)

    near = [(xs, ys), (ys, xs)]
    lo, hi = pl.ds(0, HP), pl.ds(HP, HP)

    def index(name, h, i, count, k):
        return SEM[name] + (h * PARTS + i) * count + k

    def to_mate(h, i, k):
        rows = (pl.ds(0, 1), pl.ds(1, 2), pl.ds(3, 1))[k]
        send(sib_s.at[h, i, rows], sib_r.at[h, i, rows], index("sib", h, i, 3, k), mate)

    def from_mate(h, i, k):
        rows = (pl.ds(0, 1), pl.ds(1, 2), pl.ds(3, 1))[k]
        arrived(sib_r.at[h, i, rows], index("sib", h, i, 3, k))

    def product(i):
        for h in range(2):
            right = wf[h, 4 * i : 4 * i + 4].reshape(PART, COLS)
            out = dot(gj[h].reshape(PLANE, COLS), right, 1, 1).reshape(2, 4, 4, 16, PART)
            sib_s[h, i] = out[1].astype(BF16)
            own[h, i] = out[0]
        for h in range(2):
            to_mate(h, i, 0)
            if i > 0:
                to_mate(h, i - 1, 1)
            if i == PARTS - 1:
                to_mate(h, i, 1)
                for k in range(PARTS):
                    to_mate(h, k, 2)

    def stage_far(i):
        for h in range(2):
            from_mate(h, i, 0)
            far[h, i] = (own[h, i, 0] + sib_r[h, i, 0].astype(F32)).astype(BF16)
            send(far.at[h, i, :, :, lo], r1.at[h, i, 0], index("r1", h, i, 2, 0), near[h][0][0])
            send(far.at[h, i, :, :, hi], r1.at[h, i, 1], index("r1", h, i, 2, 1), near[h][0][2])

    def stage_near(i):
        for h in range(2):
            from_mate(h, i, 1)
            for k in range(2):
                arrived(r1.at[h, i, k], index("r1", h, i, 2, k))
                both = own[h, i, 1 + k] + sib_r[h, i, 1 + k].astype(F32)
                more = r1[h, i, k].astype(F32)
                if k == 0:
                    beside[h, i, k, :, :, 0:HP] = (both[:, :, 0:HP] + more).astype(BF16)
                    beside[h, i, k, :, :, HP:PART] = both[:, :, HP:PART].astype(BF16)
                else:
                    beside[h, i, k, :, :, 0:HP] = both[:, :, 0:HP].astype(BF16)
                    beside[h, i, k, :, :, HP:PART] = (both[:, :, HP:PART] + more).astype(BF16)
                send(beside.at[h, i, k], r2.at[h, i, k], index("r2", h, i, 2, k), near[h][0][2 * k])

    def columns(h, i):
        return slice(HALF * h + PART * i, HALF * h + PART * i + PART)

    def stage_own(i):
        for h in range(2):
            from_mate(h, i, 2)
            arrived(r2.at[h, i, 0], index("r2", h, i, 2, 0))
            arrived(r2.at[h, i, 1], index("r2", h, i, 2, 1))
            total = own[h, i, 3] + sib_r[h, i, 3].astype(F32) + r2[h, i, 0].astype(F32) + r2[h, i, 1].astype(F32)
            gn[:, columns(h, i)] += total[3]
            tot[h, i] = total[0:3].astype(BF16)
            for k, device in enumerate((near[h][1][1], near[h][1][0], near[h][1][2])):
                send(tot.at[h, i, k], r3.at[h, i, k], index("r3", h, i, 3, k), device)

    def stage_last(i):
        for h in range(2):
            for k in range(3):
                arrived(r3.at[h, i, k], index("r3", h, i, 3, k))
            more = r3[h, i].astype(F32)
            gn[:, columns(h, i)] += more[0] + more[1] + more[2]

    factor = float(SEQ * 32) ** (-0.5)

    def spread(ref, slot, name, devices):
        for d in range(3):
            send(ref.at[slot], ref.at[slot], SEM[name] + d, devices[d])

    def gathered(ref, slot, name):
        for d in range(3):
            arrived(ref.at[lax.rem(slot + 3 - d, 4)], SEM[name] + d)

    def small(step):
        if step == 0:
            arrived(gls.at[other_c], SEM["g0"])
            glx[x] = gls[0] + gls[1]
            spread(glx, x, "g1", xs)
        if step == 1:
            gathered(glx, x, "g1")
            gly[y] = glx[0] + glx[1] + glx[2] + glx[3]
            spread(gly, y, "g2", ys)
        if step == 2:
            gathered(gly, y, "g2")
            low = gly[0] + gly[1] + gly[2] + gly[3]
            low = jnp.concatenate([low, jnp.zeros((8, PLANE), F32)], axis=0).astype(BF16)
            token = lax.broadcasted_iota(jnp.int32, (16, PLANE), 0) + (yl * SEQ + tt * 16)
            column = lax.broadcasted_iota(jnp.int32, (16, PLANE), 1)
            pick = jnp.where(token == column, 1.0, 0.0).astype(BF16)
            gn[...] = dot(dot(pick, low, 1, 1).astype(BF16), dpad[...])
            lanes = pl.ds(pl.multiple_of(384 * (4 * y + x), 128), 384)
            a_part = dot(low, norm[:, :, :, :, :, lanes].reshape(PLANE, 384))[0:RANK]
            z1[zl, 0:RANK] = a_part
            z1[zl, RANK : 2 * RANK] = b_part
            spread(z1, zl, "z1", zq)
        if step == 3:
            gathered(z1, zl, "z1")
            z2[zh] = z1[0] + z1[1] + z1[2] + z1[3]
            spread(z2, zh, "z2", zs)
        if step == 4:
            gathered(z2, zh, "z2")
            total = (z2[0] + z2[1] + z2[2] + z2[3]) * factor
            ga[y, x] = total[0:RANK]
            gb[yl] = total[RANK : 2 * RANK]
            send(gb.at[yl], gb.at[yl], SEM["by"], pair)
            for k, device in enumerate(across):
                send(ga.at[y, x], ga.at[y, x], SEM["ax"] + k, device)
        if step == 5:
            arrived(gb.at[other_y], SEM["by"])
            for h in range(2):
                for j in range(3):
                    o_b[:, 256 * j + 128 * h : 256 * j + 128 * h + 128] = gb[h, :, 128 * j : 128 * j + 128]
            for k, (a, b) in enumerate(plane):
                arrived(ga.at[lax.rem(y + 4 - a, 4), lax.rem(x + 4 - b, 4)], SEM["ax"] + k)
            for a in range(4):
                for b in range(4):
                    k = 384 * (4 * a + b)
                    o_a[:, k : k + 384] = ga[a, b]

    product(0)
    product(1)
    stage_far(0)
    small(0)
    product(2)
    stage_far(1)
    product(3)
    stage_far(2)
    stage_far(3)
    small(1)
    for i in range(PARTS):
        stage_near(i)
    flush(40)
    small(2)
    stage_own(0)
    small(3)
    stage_own(1)
    stage_last(0)
    small(4)
    flush(34)
    stage_own(2)
    stage_last(1)
    flush(24)
    stage_own(3)
    stage_last(2)
    flush(12)
    small(5)
    stage_last(3)

    def finish():
        get_og.wait()
        gradient = gn[...] * gain[...]
        out = norm_backward(gradient, xhat[...], inv[:, 0:1])
        o_tok[...] = (og[...].astype(F32) + out).astype(BF16)

    finish()
    flush()


def copies(a, b, d, o_a, o_b, o_d):
    o_a[...] = a[...]
    o_b[...] = b[...]
    o_d[...] = d[...]


def per_device(tokens, gain, weight, down, up, out_gradient, att_gradient):
    vmem = pl.BlockSpec(memory_space=pltpu.VMEM)
    shapes = [
        ((16, WIDTH), BF16),
        ((1, WIDTH), F32),
        ((RANK, WIDTH), BF16),
        ((RANK, 2 * COLS), BF16),
        ((16, WIDTH), BF16),
        ((2, 2, 4, 2, 16, WIDTH), BF16),
        ((2, NZ, ROWS, COLS), BF16),
        ((PLANE, COLS), F32),
        ((2, SEQ, HEAD), BF16),
        ((16, WIDTH), F32),
        ((16, HEAD), F32),
        ((16, WIDTH), BF16),
        ((16, COLS), BF16),
        ((PLANE, 16), BF16),
        ((2, 2, 4, 4, 16, COLS), BF16),
        ((2, PARTS, 4, 4, 16, PART), BF16),
        ((2, PARTS, 4, 4, 16, PART), BF16),
        ((2, PARTS, 4, 4, 16, PART), F32),
        ((2, PARTS, 4, 16, PART), BF16),
        ((2, PARTS, 2, 4, 16, HP), BF16),
        ((2, PARTS, 2, 4, 16, PART), BF16),
        ((2, PARTS, 2, 4, 16, PART), BF16),
        ((2, PARTS, 3, 16, PART), BF16),
        ((2, PARTS, 3, 16, PART), BF16),
        ((16, WIDTH), F32),
        ((2, RANK, PLANE), F32),
        ((4, RANK, PLANE), F32),
        ((4, RANK, PLANE), F32),
        ((4, 2 * RANK, COLS), F32),
        ((4, 2 * RANK, COLS), F32),
        ((4, 4, RANK, 384), F32),
        ((2, RANK, COLS), F32),
    ]
    scratch = [pltpu.VMEM(shape, kind) for shape, kind in shapes]
    scratch += [pltpu.SemaphoreType.DMA((N_SEM,)), pltpu.SemaphoreType.DMA((N_SEM,)), pltpu.SemaphoreType.DMA((9,))]
    out_shape = (
        jax.ShapeDtypeStruct((16, WIDTH), BF16),
        jax.ShapeDtypeStruct((RANK, WIDTH), F32),
        jax.ShapeDtypeStruct((RANK, 2 * COLS), F32),
    )
    results = pl.pallas_call(
        kernel,
        out_shape=out_shape,
        in_specs=[pl.BlockSpec(memory_space=pltpu.HBM)] * 7,
        out_specs=(vmem, vmem, vmem),
        scratch_shapes=scratch,
        compiler_params=pltpu.CompilerParams(
            collective_id=0, has_side_effects=True, vmem_limit_bytes=60 * 1024 * 1024
        ),
    )(tokens, gain.reshape(1, WIDTH), weight, down, up, out_gradient, att_gradient)
    return pl.pallas_call(
        copies,
        out_shape=out_shape,
        in_specs=[vmem] * 3,
        out_specs=(vmem, vmem, vmem),
    )(*results)


def solution(mesh):
    placed = (
        P(("dp", "tensor"), None),
        P(),
        P("dp", "tensor"),
        P(),
        P(None, "tensor"),
        P(("dp", "tensor"), None),
        P("dp", "tensor"),
    )
    return jax.shard_map(
        per_device,
        mesh=mesh,
        in_specs=placed,
        out_specs=(P(("dp", "tensor"), None), P(), P(None, "tensor")),
        check_vma=False,
    )
```

time: 121 us -> 109 us (0.901)
  the two profiles are of different devices: /device:TPU:32 before, /device:TPU:2 now
where the time goes in v2:
time: 109 us
  Pallas kernels  108 us (99%)
    pallas_call x1, Pallas kernels, per_device(): pl.pallas_call(kernel, out_shape=out_shape, in_specs=[pl.BlockSpec(memory...  106 us

profile of v2, /device:TPU:2, one launch (start us, length us, event | category | flops | bytes accessed | tf_op | source)
XLA Modules:
  0.0 108.8 jit_solution(11402438277111287394)
XLA Ops:
  0.6 106.3 %shard_map.94 = (bf16[16,6144]{1,0:T(8,128)(2,1)}, f32[8,6144]{1,0:T(8,128)}, f32[8,768]{1,0:T(8,128)}) custom-call(bf16[16,6144]{1,0:T(8,128)(2,1)} %tok_in.1, f32[1,6144]{1,0:T(1,128)} %bitcast.1, bf16[192,768]{1,0:T(8,128)(2,1)} %w_in.1, bf16[8,6144]{1,0:T(8,128)(2,1)} %down_in.1, bf16[8,768]{1,0:T(8,128)(2,1)} %up_in.1, bf16[16,6144]{1,0:T(8,128)(2,1)} %og_in.1, ...), custom_call_target="tpu_custom_call" | custom-call | tf_op jit(solution)/shard_map/pallas_call | solution.py:542
  107.0 1.8 %shard_map.95 = (bf16[16,6144]{1,0:T(8,128)(2,1)}, f32[8,6144]{1,0:T(8,128)}, f32[8,768]{1,0:T(8,128)}) custom-call(bf16[16,6144]{1,0:T(8,128)(2,1)} %get-tuple-element.6.a, f32[8,6144]{1,0:T(8,128)} %get-tuple-element.7.b, f32[8,768]{1,0:T(8,128)} %get-tuple-element.8.d), custom_call_target="tpu_custom_call" | custom-call | tf_op jit(solution)/shard_map/pallas_call | solution.py:552

commit v3 on v2

--- a/solution.py
+++ b/solution.py
@@ -54,8 +54,8 @@
 def plan():
     al = Allocator()
     names = dict(
-        wy=3, do=1, ring=32, t1=6, t2=6, t3=2,
-        sib=6 * PARTS, r1=4 * PARTS, r2=4 * PARTS, r3=6 * PARTS,
+        wy=6, do=1, ring=64, t1=6, t2=6, t3=2,
+        sib=4 * PARTS, r1=4 * PARTS, r2=4 * PARTS, r3=6 * PARTS,
         g0=1, g1=3, g2=3, z1=3, z2=3, ax=15, by=1,
     )
     bases = {name: al.take(count) for name, count in names.items()}
@@ -101,7 +101,8 @@
     pair = at(2 * yh + other_y, x, z, c)
     plane = [(a, b) for a in range(4) for b in range(4) if a + b > 0]
     across = [at(lax.rem(y + a, 4), lax.rem(x + b, 4), z, c) for a, b in plane]
-    peers = [mate, *across, zu, zd, *zq, *zs]
+    peers = [mate, *across, zu, zd]
+    later_peers = [*zq, *zs]
 
     def copy(src, dst, k, device):
         return pltpu.make_async_remote_copy(
@@ -147,26 +148,30 @@
 
     pl.semaphore_wait(barrier, len(peers))
 
-    for j in range(3):
-        cols = pl.ds(pl.multiple_of(256 * j + other_y * HEAD, HEAD), HEAD)
-        send(w_in.at[:, cols], wf.at[yl, z, :, pl.ds(128 * j, 128)], SEM["wy"] + j, pair)
+    rows_of = (pl.ds(0, ROWS // 2), pl.ds(ROWS // 2, ROWS // 2))
+    for k in range(2):
+        for j in range(3):
+            cols = pl.ds(pl.multiple_of(256 * j + other_y * HEAD, HEAD), HEAD)
+            to = wf.at[yl, z, rows_of[k], pl.ds(128 * j, 128)]
+            send(w_in.at[rows_of[k], cols], to, SEM["wy"] + 3 * k + j, pair)
     for one in get_w:
         one.wait()
 
-    def ring_index(way, step, j):
-        return SEM["ring"] + way * 16 + (step - 1) * 2 + j
-
-    def ring_send(way, step, j):
+    def ring_index(way, step, j, k):
+        return SEM["ring"] + way * 32 + (step - 1) * 4 + 2 * j + k
+
+    def ring_send(way, step, j, k):
         block = lax.rem(z + NZ - (step - 1), NZ) if way == 0 else lax.rem(z + step - 1, NZ)
-        ref = wf.at[j, block]
-        send(ref, ref, ring_index(way, step, j), zu if way == 0 else zd)
-
-    def ring_wait(way, step, j):
+        ref = wf.at[j, block, rows_of[k]]
+        send(ref, ref, ring_index(way, step, j, k), zu if way == 0 else zd)
+
+    def ring_wait(way, step, j, k):
         block = lax.rem(z + NZ - step, NZ) if way == 0 else lax.rem(z + step, NZ)
-        arrived(wf.at[j, block], ring_index(way, step, j))
-
-    for way in range(2):
-        ring_send(way, 1, yl)
+        arrived(wf.at[j, block, rows_of[k]], ring_index(way, step, j, k))
+
+    for k in range(2):
+        for way in range(2):
+            ring_send(way, 1, yl, k)
     for one in get_tok:
         one.wait()
     normal, inverse = row_norm(tok[...].astype(F32))
@@ -191,10 +196,14 @@
             [up[:, cols].astype(F32), jnp.zeros((8, HEAD), F32)], axis=0
         ).astype(BF16)
 
-    for j in range(3):
-        arrived(wf.at[other_y, z, :, pl.ds(128 * j, 128)], SEM["wy"] + j)
-    for way in range(2):
-        ring_send(way, 1, other_y)
+    for k in range(2):
+        for way in range(2):
+            ring_wait(way, 1, yl, k)
+            ring_send(way, 2, yl, k)
+        for j in range(3):
+            arrived(wf.at[other_y, z, rows_of[k], pl.ds(128 * j, 128)], SEM["wy"] + 3 * k + j)
+        for way in range(2):
+            ring_send(way, 1, other_y, k)
 
     def forward(step):
         up_way = lax.rem(step + z, 2)
@@ -246,20 +255,23 @@
 
     def ring_step(step):
         if step < 8:
-            for j in (yl, other_y):
+            for j in (yl, other_y) if step > 2 else (other_y,):
+                for k in range(2):
+                    for way in range(2):
+                        ring_wait(way, step - 1, j, k)
+                        ring_send(way, step, j, k)
+        elif step == 8:
+            for k in range(2):
                 for way in range(2):
-                    ring_wait(way, step - 1, j)
-                    ring_send(way, step, j)
-        elif step == 8:
-            ring_wait(0, 7, 0)
-            ring_send(0, 8, 0)
-            ring_wait(1, 7, 1)
-            ring_send(1, 8, 1)
-            ring_wait(0, 7, 1)
-            ring_wait(1, 7, 0)
+                    ring_wait(way, 7, way, k)
+                    ring_send(way, 8, way, k)
+            for k in range(2):
+                for way in range(2):
+                    ring_wait(way, 7, 1 - way, k)
         else:
-            ring_wait(0, 8, 0)
-            ring_wait(1, 8, 1)
+            for k in range(2):
+                for way in range(2):
+                    ring_wait(way, 8, way, k)
 
     def dout_done():
         arrived(dall.at[other_y], SEM["do"])
@@ -269,18 +281,20 @@
         ring_step(step)
         if step == 2:
             tokens_second()
-        if step == 5:
+        if step == 6:
             tokens_mate()
-        if step == 6:
+        if step == 7:
             tokens_done()
             forward_first()
-        if step == 7:
+        if step == 8:
             forward(6)
-        if step == 8:
             forward(7)
             dout_done()
         if step == 9:
             forward(8)
+
+    for device in later_peers:
+        pl.semaphore_signal(barrier, inc=1, device_id=device, device_id_type=pl.DeviceIdType.MESH)
 
     def order(to, me):
         d = lax.rem(to - me + 6, 4)
@@ -330,12 +344,12 @@
         return SEM[name] + (h * PARTS + i) * count + k
 
     def to_mate(h, i, k):
-        rows = (pl.ds(0, 1), pl.ds(1, 2), pl.ds(3, 1))[k]
-        send(sib_s.at[h, i, rows], sib_r.at[h, i, rows], index("sib", h, i, 3, k), mate)
+        rows = (pl.ds(0, 1), pl.ds(1, 3))[k]
+        send(sib_s.at[h, i, rows], sib_r.at[h, i, rows], index("sib", h, i, 2, k), mate)
 
     def from_mate(h, i, k):
-        rows = (pl.ds(0, 1), pl.ds(1, 2), pl.ds(3, 1))[k]
-        arrived(sib_r.at[h, i, rows], index("sib", h, i, 3, k))
+        rows = (pl.ds(0, 1), pl.ds(1, 3))[k]
+        arrived(sib_r.at[h, i, rows], index("sib", h, i, 2, k))
 
     def product(i):
         for h in range(2):
@@ -349,8 +363,6 @@
                 to_mate(h, i - 1, 1)
             if i == PARTS - 1:
                 to_mate(h, i, 1)
-                for k in range(PARTS):
-                    to_mate(h, k, 2)
 
     def stage_far(i):
         for h in range(2):
@@ -379,7 +391,6 @@
 
     def stage_own(i):
         for h in range(2):
-            from_mate(h, i, 2)
             arrived(r2.at[h, i, 0], index("r2", h, i, 2, 0))
             arrived(r2.at[h, i, 1], index("r2", h, i, 2, 1))
             total = own[h, i, 3] + sib_r[h, i, 3].astype(F32) + r2[h, i, 0].astype(F32) + r2[h, i, 1].astype(F32)
@@ -388,12 +399,18 @@
             for k, device in enumerate((near[h][1][1], near[h][1][0], near[h][1][2])):
                 send(tot.at[h, i, k], r3.at[h, i, k], index("r3", h, i, 3, k), device)
 
+    sums = [0.0, 0.0]
+
     def stage_last(i):
         for h in range(2):
             for k in range(3):
                 arrived(r3.at[h, i, k], index("r3", h, i, 3, k))
             more = r3[h, i].astype(F32)
-            gn[:, columns(h, i)] += more[0] + more[1] + more[2]
+            cols = columns(h, i)
+            grad = (gn[:, cols] + (more[0] + more[1] + more[2])) * gain[:, cols]
+            gn[:, cols] = grad
+            sums[0] += jnp.sum(grad, axis=-1, keepdims=True)
+            sums[1] += jnp.sum(grad * xhat[:, cols], axis=-1, keepdims=True)
 
     factor = float(SEQ * 32) ** (-0.5)
 
@@ -426,6 +443,7 @@
             a_part = dot(low, norm[:, :, :, :, :, lanes].reshape(PLANE, 384))[0:RANK]
             z1[zl, 0:RANK] = a_part
             z1[zl, RANK : 2 * RANK] = b_part
+            pl.semaphore_wait(barrier, len(later_peers))
             spread(z1, zl, "z1", zq)
         if step == 3:
             gathered(z1, zl, "z1")
@@ -468,22 +486,21 @@
     stage_own(0)
     small(3)
     stage_own(1)
+    stage_own(2)
+    small(4)
+    stage_own(3)
+    flush(54)
     stage_last(0)
-    small(4)
-    flush(34)
-    stage_own(2)
     stage_last(1)
+    small(5)
     flush(24)
-    stage_own(3)
     stage_last(2)
-    flush(12)
-    small(5)
     stage_last(3)
 
     def finish():
         get_og.wait()
-        gradient = gn[...] * gain[...]
-        out = norm_backward(gradient, xhat[...], inv[:, 0:1])
+        first, second = sums[0] * (1.0 / WIDTH), sums[1] * (1.0 / WIDTH)
+        out = (gn[...] - first - xhat[...] * second) * inv[:, 0:1]
         o_tok[...] = (og[...].astype(F32) + out).astype(BF16)
 
     finish()
@@ -498,6 +515,7 @@
 
 def per_device(tokens, gain, weight, down, up, out_gradient, att_gradient):
     vmem = pl.BlockSpec(memory_space=pltpu.VMEM)
+    hbm = pl.BlockSpec(memory_space=pltpu.HBM)
     shapes = [
         ((16, WIDTH), BF16),
         ((1, WIDTH), F32),
@@ -542,7 +560,7 @@
     results = pl.pallas_call(
         kernel,
         out_shape=out_shape,
-        in_specs=[pl.BlockSpec(memory_space=pltpu.HBM)] * 7,
+        in_specs=[hbm] * 7,
         out_specs=(vmem, vmem, vmem),
         scratch_shapes=scratch,
         compiler_params=pltpu.CompilerParams(

time: 109 us -> 106 us (0.972)
  the two profiles are of different devices: /device:TPU:2 before, /device:TPU:8 now
where the time goes in v3:
time: 106 us
  Pallas kernels  106 us (100%)
    pallas_call x1, Pallas kernels, per_device(): pl.pallas_call(kernel, out_shape=out_shape, in_specs=[hbm] * 7, out_specs...  104 us

profile of v3, /device:TPU:8, one launch (start us, length us, event | category | flops | bytes accessed | tf_op | source)
XLA Modules:
  0.0 106.3 jit_solution(10302479982947717600)
XLA Ops:
  0.6 103.9 %shard_map.94 = (bf16[16,6144]{1,0:T(8,128)(2,1)}, f32[8,6144]{1,0:T(8,128)}, f32[8,768]{1,0:T(8,128)}) custom-call(bf16[16,6144]{1,0:T(8,128)(2,1)} %tok_in.1, f32[1,6144]{1,0:T(1,128)} %bitcast.1, bf16[192,768]{1,0:T(8,128)(2,1)} %w_in.1, bf16[8,6144]{1,0:T(8,128)(2,1)} %down_in.1, bf16[8,768]{1,0:T(8,128)(2,1)} %up_in.1, bf16[16,6144]{1,0:T(8,128)(2,1)} %og_in.1, ...), custom_call_target="tpu_custom_call" | custom-call | tf_op jit(solution)/shard_map/pallas_call | solution.py:560
  104.6 1.8 %shard_map.95 = (bf16[16,6144]{1,0:T(8,128)(2,1)}, f32[8,6144]{1,0:T(8,128)}, f32[8,768]{1,0:T(8,128)}) custom-call(bf16[16,6144]{1,0:T(8,128)(2,1)} %get-tuple-element.6.a, f32[8,6144]{1,0:T(8,128)} %get-tuple-element.7.b, f32[8,768]{1,0:T(8,128)} %get-tuple-element.8.d), custom_call_target="tpu_custom_call" | custom-call | tf_op jit(solution)/shard_map/pallas_call | solution.py:570

commit v4 on v3

--- a/solution.py
+++ b/solution.py
@@ -13,6 +13,7 @@
 NZ = 16
 ROWS = 192
 COLS = 3 * HEAD
+PIECES = 1
 PARTS = 4
 PART = HALF // PARTS
 HP = PART // 2
@@ -146,10 +147,28 @@
     get_small = [fetch(down_in, down), fetch(up_in, up), fetch(dout_in.at[:, own_cols], dall.at[yl])]
     get_og = fetch(og_in, og)
 
+    for one in get_tok:
+        one.wait()
+    normal, inverse = row_norm(tok[...].astype(F32))
+    xhat[...] = normal
+    inv[...] = jnp.broadcast_to(inverse, inv.shape)
+    norm[yl, yh, x, c] = (normal * gain[...]).astype(BF16)
+
+    for one in get_small:
+        one.wait()
+
+    dpad[...] = jnp.concatenate([down[...].astype(F32), jnp.zeros((8, WIDTH), F32)], axis=0).astype(BF16)
+    for j in range(3):
+        cols = pl.ds(pl.multiple_of(256 * j + yl * HEAD, HEAD), HEAD)
+        upad[:, 128 * j : 128 * j + 128] = jnp.concatenate(
+            [up[:, cols].astype(F32), jnp.zeros((8, HEAD), F32)], axis=0
+        ).astype(BF16)
+
     pl.semaphore_wait(barrier, len(peers))
 
-    rows_of = (pl.ds(0, ROWS // 2), pl.ds(ROWS // 2, ROWS // 2))
-    for k in range(2):
+    piece = ROWS // PIECES
+    rows_of = [pl.ds(piece * k, piece) for k in range(PIECES)]
+    for k in range(PIECES):
         for j in range(3):
             cols = pl.ds(pl.multiple_of(256 * j + other_y * HEAD, HEAD), HEAD)
             to = wf.at[yl, z, rows_of[k], pl.ds(128 * j, 128)]
@@ -169,16 +188,9 @@
         block = lax.rem(z + NZ - step, NZ) if way == 0 else lax.rem(z + step, NZ)
         arrived(wf.at[j, block, rows_of[k]], ring_index(way, step, j, k))
 
-    for k in range(2):
+    for k in range(PIECES):
         for way in range(2):
             ring_send(way, 1, yl, k)
-    for one in get_tok:
-        one.wait()
-    normal, inverse = row_norm(tok[...].astype(F32))
-    xhat[...] = normal
-    inv[...] = jnp.broadcast_to(inverse, inv.shape)
-    norm[yl, yh, x, c] = (normal * gain[...]).astype(BF16)
-
     a_cols, b_cols = pl.ds(0, HALF), pl.ds(HALF, HALF)
     a_ref = norm.at[yl, yh, x, c, :, a_cols]
     b_ref = norm.at[yl, yh, x, c, :, b_cols]
@@ -186,17 +198,7 @@
         send(a_ref, a_ref, SEM["t1"] + d, xs[d])
         send(b_ref, b_ref, SEM["t1"] + 3 + d, ys[d])
     send(dout_in.at[:, pair_cols], dall.at[yl], SEM["do"], pair)
-    for one in get_small:
-        one.wait()
-
-    dpad[...] = jnp.concatenate([down[...].astype(F32), jnp.zeros((8, WIDTH), F32)], axis=0).astype(BF16)
-    for j in range(3):
-        cols = pl.ds(pl.multiple_of(256 * j + yl * HEAD, HEAD), HEAD)
-        upad[:, 128 * j : 128 * j + 128] = jnp.concatenate(
-            [up[:, cols].astype(F32), jnp.zeros((8, HEAD), F32)], axis=0
-        ).astype(BF16)
-
-    for k in range(2):
+    for k in range(PIECES):
         for way in range(2):
             ring_wait(way, 1, yl, k)
             ring_send(way, 2, yl, k)
@@ -209,11 +211,12 @@
         up_way = lax.rem(step + z, 2)
         base = lax.rem(up_way * (z + step - 1) + (1 - up_way) * (z - step + NZ), NZ)
         block = lax.div(base, 2)
+        left = []
         for j in range(2):
             lanes = pl.ds(pl.multiple_of(HALF * j + 2 * ROWS * block, 128), 2 * ROWS)
-            left = norm[:, :, :, :, :, lanes].reshape(PLANE, 2 * ROWS)
-            right = wf[j, pl.ds(2 * block, 2)].reshape(2 * ROWS, COLS)
-            acc[...] += dot(left, right)
+            left.append(norm[:, :, :, :, :, lanes].reshape(PLANE, 2 * ROWS))
+        right = wf[:, pl.ds(2 * block, 2)].reshape(4 * ROWS, COLS)
+        acc[...] += dot(jnp.concatenate(left, axis=1), right)
 
     def tokens_second():
         for d in range(3):
@@ -251,25 +254,25 @@
             forward(s)
             return carry
 
-        lax.fori_loop(1, 6, several, 0)
+        lax.fori_loop(1, 4, several, 0)
 
     def ring_step(step):
         if step < 8:
             for j in (yl, other_y) if step > 2 else (other_y,):
-                for k in range(2):
+                for k in range(PIECES):
                     for way in range(2):
                         ring_wait(way, step - 1, j, k)
                         ring_send(way, step, j, k)
         elif step == 8:
-            for k in range(2):
+            for k in range(PIECES):
                 for way in range(2):
                     ring_wait(way, 7, way, k)
                     ring_send(way, 8, way, k)
-            for k in range(2):
+            for k in range(PIECES):
                 for way in range(2):
                     ring_wait(way, 7, 1 - way, k)
         else:
-            for k in range(2):
+            for k in range(PIECES):
                 for way in range(2):
                     ring_wait(way, 8, way, k)
 
@@ -287,8 +290,8 @@
             tokens_done()
             forward_first()
         if step == 8:
-            forward(6)
-            forward(7)
+            for pair_step in range(4, 8):
+                forward(pair_step)
             dout_done()
         if step == 9:
             forward(8)

time: 106 us -> 106 us (level)
  no operation moved by 1% of the time
where the time goes in v4:
time: 106 us
  Pallas kernels  105 us (99%)
    pallas_call x1, Pallas kernels, per_device(): pl.pallas_call(kernel, out_shape=out_shape, in_specs=[hbm] * 7, out_specs...  104 us

profile of v4, /device:TPU:8, one launch (start us, length us, event | category | flops | bytes accessed | tf_op | source)
XLA Modules:
  0.0 105.9 jit_solution(14439994325603741571)
XLA Ops:
  0.6 103.5 %shard_map.94 = (bf16[16,6144]{1,0:T(8,128)(2,1)}, f32[8,6144]{1,0:T(8,128)}, f32[8,768]{1,0:T(8,128)}) custom-call(bf16[16,6144]{1,0:T(8,128)(2,1)} %tok_in.1, f32[1,6144]{1,0:T(1,128)} %bitcast.1, bf16[192,768]{1,0:T(8,128)(2,1)} %w_in.1, bf16[8,6144]{1,0:T(8,128)(2,1)} %down_in.1, bf16[8,768]{1,0:T(8,128)(2,1)} %up_in.1, bf16[16,6144]{1,0:T(8,128)(2,1)} %og_in.1, ...), custom_call_target="tpu_custom_call" | custom-call | tf_op jit(solution)/shard_map/pallas_call | solution.py:563
  104.2 1.8 %shard_map.95 = (bf16[16,6144]{1,0:T(8,128)(2,1)}, f32[8,6144]{1,0:T(8,128)}, f32[8,768]{1,0:T(8,128)}) custom-call(bf16[16,6144]{1,0:T(8,128)(2,1)} %get-tuple-element.6.a, f32[8,6144]{1,0:T(8,128)} %get-tuple-element.7.b, f32[8,768]{1,0:T(8,128)} %get-tuple-element.8.d), custom_call_target="tpu_custom_call" | custom-call | tf_op jit(solution)/shard_map/pallas_call | solution.py:573

commit v5 on v4

--- a/solution.py
+++ b/solution.py
@@ -305,27 +305,27 @@
 
     scale = HEAD ** (-0.5)
     def attention():
-        for i in range(2):
-            rows = slice(SEQ * i, SEQ * i + SEQ)
-            q_norm, q_inv = row_norm(acc[rows, 0:128])
-            k_norm, k_inv = row_norm(acc[rows, 128:256])
-            value = acc[rows, 256:384].astype(BF16)
-            query, key = q_norm.astype(BF16), k_norm.astype(BF16)
-            weights = jnp.exp(dot(query, key, 1, 1) * scale)
-            probs = weights / jnp.sum(weights, axis=-1, keepdims=True)
-            cot = dall[i]
-            g_value = dot(probs.astype(BF16), cot, 0, 0)
-            g_probs = dot(cot, value, 1, 1)
-            g_scores = probs * (g_probs - jnp.sum(probs * g_probs, axis=-1, keepdims=True))
-            g_scores = (g_scores * scale).astype(BF16)
-            g_query = norm_backward(dot(g_scores, key), q_norm, q_inv)
-            g_key = norm_backward(dot(g_scores, query, 0, 0), k_norm, k_inv)
-            joined = jnp.concatenate([g_query, g_key, g_value], axis=1).astype(BF16)
-            gls[c, :, SEQ * i : SEQ * i + SEQ] = dot(upad[...], joined, 1, 1)[0:RANK]
-            if i == 0:
-                b_part = dot(lowr[rows], joined, 0, 0)
-            else:
-                b_part = b_part + dot(lowr[rows], joined, 0, 0)
+        images = range(2)
+        rows = [slice(SEQ * i, SEQ * i + SEQ) for i in images]
+        q = [row_norm(acc[r, 0:128]) for r in rows]
+        k = [row_norm(acc[r, 128:256]) for r in rows]
+        value = [acc[r, 256:384].astype(BF16) for r in rows]
+        query = [q[i][0].astype(BF16) for i in images]
+        key = [k[i][0].astype(BF16) for i in images]
+        weights = [jnp.exp(dot(query[i], key[i], 1, 1) * scale) for i in images]
+        g_probs = [dot(dall[i], value[i], 1, 1) for i in images]
+        probs = [weights[i] / jnp.sum(weights[i], axis=-1, keepdims=True) for i in images]
+        g_value = [dot(probs[i].astype(BF16), dall[i], 0, 0) for i in images]
+        inner = [jnp.sum(probs[i] * g_probs[i], axis=-1, keepdims=True) for i in images]
+        g_scores = [(probs[i] * (g_probs[i] - inner[i]) * scale).astype(BF16) for i in images]
+        g_query = [norm_backward(dot(g_scores[i], key[i]), *q[i]) for i in images]
+        g_key = [norm_backward(dot(g_scores[i], query[i], 0, 0), *k[i]) for i in images]
+        joined = [
+            jnp.concatenate([g_query[i], g_key[i], g_value[i]], axis=1).astype(BF16) for i in images
+        ]
+        for i in images:
+            gls[c, :, SEQ * i : SEQ * i + SEQ] = dot(upad[...], joined[i], 1, 1)[0:RANK]
+        for i in images:
             for bh in range(2):
                 for bx in range(4):
                     for bc in range(2):
@@ -333,8 +333,9 @@
                         by = 2 * bh + i
                         rel = lax.rem(c + bc, 2)
                         kx, ky = order(bx, x), order(by, y)
-                        gj[0, rel, kx, ky] = joined[r : r + 16]
-                        gj[1, rel, ky, kx] = joined[r : r + 16]
+                        gj[0, rel, kx, ky] = joined[i][r : r + 16]
+                        gj[1, rel, ky, kx] = joined[i][r : r + 16]
+        b_part = dot(lowr[rows[0]], joined[0], 0, 0) + dot(lowr[rows[1]], joined[1], 0, 0)
         return b_part[0:RANK]
 
     b_part = attention()

time: 106 us -> 106 us (level)
  no operation moved by 1% of the time
where the time goes in v5:
time: 106 us
  Pallas kernels  105 us (99%)
    pallas_call x1, Pallas kernels, per_device(): pl.pallas_call(kernel, out_shape=out_shape, in_specs=[hbm] * 7, out_specs...  103 us

profile of v5, /device:TPU:8, one launch (start us, length us, event | category | flops | bytes accessed | tf_op | source)
XLA Modules:
  0.0 105.5 jit_solution(3108854466792692954)
XLA Ops:
  0.6 103.1 %shard_map.94 = (bf16[16,6144]{1,0:T(8,128)(2,1)}, f32[8,6144]{1,0:T(8,128)}, f32[8,768]{1,0:T(8,128)}) custom-call(bf16[16,6144]{1,0:T(8,128)(2,1)} %tok_in.1, f32[1,6144]{1,0:T(1,128)} %bitcast.1, bf16[192,768]{1,0:T(8,128)(2,1)} %w_in.1, bf16[8,6144]{1,0:T(8,128)(2,1)} %down_in.1, bf16[8,768]{1,0:T(8,128)(2,1)} %up_in.1, bf16[16,6144]{1,0:T(8,128)(2,1)} %og_in.1, ...), custom_call_target="tpu_custom_call" | custom-call | tf_op jit(solution)/shard_map/pallas_call | solution.py:564
  103.7 1.8 %shard_map.95 = (bf16[16,6144]{1,0:T(8,128)(2,1)}, f32[8,6144]{1,0:T(8,128)}, f32[8,768]{1,0:T(8,128)}) custom-call(bf16[16,6144]{1,0:T(8,128)(2,1)} %get-tuple-element.6.a, f32[8,6144]{1,0:T(8,128)} %get-tuple-element.7.b, f32[8,768]{1,0:T(8,128)} %get-tuple-element.8.d), custom_call_target="tpu_custom_call" | custom-call | tf_op jit(solution)/shard_map/pallas_call | solution.py:574
